TPU v7x, 128 devices: a whole 4x4x4 slice. The times are simulated.
128 devices in a mesh: ctx: 4 (over y_hi, core), seq: 32 (over y_lo, z, x).
Axes of the slice: x: 4, y: 4 (y_hi: 2, y_lo: 2; y = y_hi * 2 + y_lo), z: 4, core: 2. Of those that a mesh axis runs over, the one named last changes fastest.
Arguments:
- bottom_codes: int32 [4, 32768], P(None, ('ctx', 'seq')), may hold values from 0 to 2047
- cond_codes: int32 [4, 8192], P(None, ('ctx', 'seq')), may hold values from 0 to 2047
- bottom_table: bfloat16 [2048, 1024], replicated, may hold values from -4.1875 to 4.1875
- cond_table: bfloat16 [2048, 1024], replicated, may hold values from -4.1875 to 4.1875
- conv_dilated: bfloat16 [3, 1024, 1024], replicated, may hold values from -0.109375 to 0.109375
- conv_mix: bfloat16 [1024, 1024], replicated, may hold values from -0.1875 to 0.1875
- projection: bfloat16 [1024, 1920], replicated, may hold values from -0.1875 to 0.1875
- norm_gain: float32 [1920], replicated, may hold values from 0.5 to 1.5
- norm_bias: float32 [1920], replicated, may hold values from -3 to 3
- attn_weight: bfloat16 [1920, 1440], replicated
Outputs:
- attended: bfloat16 [4, 32768, 480], P(None, ('ctx', 'seq'))
All inputs are finite; a program needn't handle non-finite values.
Results may differ from a plain program's by a relative error of at most 0.0065.
Values may be sent and summed in bfloat16 or wider, within the bound.
A program may use at most 128 MiB of HBM per device.

v0:
```python
import functools
import math

import jax
import jax.numpy as jnp
from jax import lax
from jax.experimental import pallas as pl
from jax.experimental.pallas import tpu as pltpu
from jax.sharding import PartitionSpec as P

F32, BF16, I32 = jnp.float32, jnp.bfloat16, jnp.int32
MESH = pl.DeviceIdType.MESH

BLOCK = 128
DIL_BLOCKS, DIL_REST = divmod(2187, BLOCK)
CTX, SEQ = 4, 32
ROWS = 256
HALO = 9
SLOTS = SEQ + 2 * HALO
BLOCKS = 64
COLS = 8
CHUNK = BLOCKS * COLS
VOCAB, CH, WIDTH, ATTN = 2048, 1024, 1920, 480
GROUPS = CH // 128
NOWHERE = VOCAB * 8
STAGE = 512
OWN, LEFT, RIGHT = 0, 8, 16
COND = 32
TAPS = (
    (LEFT, (0, 0, 0, 1, 1, 1, 1, 2)),
    (OWN, (0, 0, 0, 0, 1, 1, 1, 1)),
    (RIGHT, (0, 1, 1, 1, 1, 2, 2, 2)),
)


def kernel(
    bottom_ref, cond_ref, gain_ref, bias_ref, btab, ctab, conv, mix, proj, attn,
    out_ref,
    tb, tc, stage, wconv, wmix, wproj, wattn,
    sendc, codes, gath, gsm,
    act, lhs, hidden, resid, pj, normed, qkv, att, sendo,
    stage_sem, w_sem, csend_sem, crecv_sem, g_sem, osend_sem, orecv_sem, local_sem,
):
    a = lax.axis_index("ctx")
    j = lax.axis_index("seq")
    k = j // 2
    h = j % 2

    to_next = jnp.logical_and(a < CTX - 1, j >= SEQ - HALO)
    to_prev = jnp.logical_and(a > 0, j < HALO)

    barrier = pltpu.get_barrier_semaphore()

    def greet(t, _):
        pl.semaphore_signal(
            barrier, inc=1, device_id=(a, lax.rem(j + t, SEQ)), device_id_type=MESH
        )
        return 0

    lax.fori_loop(1, SEQ, greet, 0)

    @pl.when(a > 0)
    def _():
        def f(t, _):
            pl.semaphore_signal(barrier, inc=1, device_id=(a - 1, t), device_id_type=MESH)
            return 0

        lax.fori_loop(SEQ - HALO, SEQ, f, 0)

    @pl.when(a < CTX - 1)
    def _():
        def f(t, _):
            pl.semaphore_signal(barrier, inc=1, device_id=(a + 1, t), device_id_type=MESH)
            return 0

        lax.fori_loop(0, HALO, f, 0)

    def stage_copy(i):
        table = (btab, ctab)[i // 4]
        return pltpu.make_async_copy(
            table.at[pl.ds((i % 4) * STAGE, STAGE)], stage.at[i % 4], stage_sem.at[i % 4]
        )

    weights = [
        pltpu.make_async_copy(src, dst, w_sem.at[i])
        for i, (src, dst) in enumerate(
            ((conv, wconv), (mix, wmix), (proj, wproj), (attn, wattn))
        )
    ]
    for i in range(4):
        stage_copy(i).start()

    sendc[...] = jnp.zeros_like(sendc)
    for song in range(4):
        p, s = divmod(song, 2)
        for u in range(2):
            sendc[p, 2 * s + u : 2 * s + u + 1, :] = bottom_ref[
                song : song + 1, u * 128 : (u + 1) * 128
            ]
            sendc[p, 4 + s : 5 + s, u * 64 : (u + 1) * 64] = cond_ref[song : song + 1, :]

    def widen(i):
        table = (tb, tc)[i // 4]
        stage_copy(i).wait()

        def f(r, _):
            x = stage[i % 4, pl.ds(r * 16, 16), :].astype(F32)
            base = ((i % 4) * STAGE + r * 16) * 8
            for q in range(2):
                for g in range(GROUPS):
                    table[pl.ds(base + q * 64 + g, 8, stride=8), :] = x[
                        8 * q : 8 * q + 8, 128 * g : 128 * g + 128
                    ]
            return 0

        lax.fori_loop(0, STAGE // 16, f, 0, unroll=2)
        if i + 4 < 8:
            stage_copy(i + 4).start()

    for i in range(4):
        widen(i)
    for w in weights:
        w.start()
    tb[pl.ds(NOWHERE, 8), :] = jnp.full((8, 128), -1e9, F32)

    pl.semaphore_wait(barrier, SEQ - 1 + jnp.where(jnp.logical_or(to_next, to_prev), SEQ, 0))

    def send_codes(ctx, peer, slot, sem):
        pltpu.make_async_remote_copy(
            src_ref=sendc.at[peer % 2],
            dst_ref=codes.at[slot],
            send_sem=csend_sem,
            recv_sem=crecv_sem.at[sem],
            device_id=(ctx, peer),
            device_id_type=MESH,
        ).start()

    def own_codes(t, _):
        send_codes(a, lax.rem(j + t, SEQ), j + HALO, 0)
        return 0

    lax.fori_loop(1, SEQ, own_codes, 0)

    @pl.when(to_next)
    def _():
        def f(t, _):
            send_codes(a + 1, t, j - (SEQ - HALO), 1)
            return 0

        lax.fori_loop(0, SEQ, f, 0)

    @pl.when(to_prev)
    def _():
        def f(t, _):
            send_codes(a - 1, t, j + SEQ + HALO, 2)
            return 0

        lax.fori_loop(0, SEQ, f, 0)

    codes[j + HALO] = sendc[h]
    outside = jnp.where(lax.broadcasted_iota(I32, (HALO, 8, 128), 1) < 4, VOCAB, 0)

    @pl.when(a == 0)
    def _():
        codes[0:HALO] = outside

    @pl.when(a == CTX - 1)
    def _():
        codes[SEQ + HALO : SLOTS] = outside

    for i in range(4, 8):
        widen(i)

    def code_wait(count, sem):
        view = codes.at[pl.ds(0, count)]
        pltpu.make_async_copy(view, view, sem).wait()

    code_wait(SEQ - 1, crecv_sem.at[0])

    @pl.when(a > 0)
    def _():
        code_wait(HALO, crecv_sem.at[1])

    @pl.when(a < CTX - 1)
    def _():
        code_wait(HALO, crecv_sem.at[2])

    lanes = lax.broadcasted_iota(I32, (BLOCKS // 2, 128), 1)
    for s in range(2):
        for v in range(2):
            def bottom(beta):
                d, u = divmod(beta, 2)
                return codes[d : d + BLOCKS // 2, 2 * s + u, :]

            def upper(beta):
                d, u = divmod(beta, 2)
                x = codes[d : d + BLOCKS // 2, 4 + s, :]
                if u:
                    y = codes[d + 1 : d + 1 + BLOCKS // 2, 4 + s, :]
                    x = jnp.where(lanes < 64, x, y)
                return x, 32 * u

            lead = v + 2 * HALO
            before, after = lead - DIL_BLOCKS, lead + DIL_BLOCKS
            left = jnp.where(lanes >= 128 - DIL_REST, bottom(before - 1), bottom(before))
            right = jnp.where(lanes < DIL_REST, bottom(after + 1), bottom(after))
            up_own, own0 = upper(lead)
            up_left, left0 = upper(before - 1)
            up_right, right0 = upper(after)
            row = None
            for x, lane0, first, step in (
                (bottom(lead), OWN, 0, COLS),
                (left, LEFT, -DIL_REST, COLS),
                (right, RIGHT, DIL_REST, COLS),
                (up_own, COND + OWN, own0, 2),
                (up_left, COND + LEFT, left0 + 32 - 3, 2),
                (up_right, COND + RIGHT, right0 + 2, 2),
            ):
                amount = lax.rem(lane0 - first + 256 - step * k, 128)
                rolled = pltpu.roll(x, amount, 1)
                row = rolled if row is None else jnp.where(lanes >= lane0, rolled, row)
            gath[pl.ds(s * BLOCKS + v, BLOCKS // 2, stride=2), :] = row
    to_smem = pltpu.make_async_copy(gath, gsm, g_sem)
    to_smem.start()
    to_smem.wait()

    for w in weights:
        w.wait()

    scale = 1.0 / math.sqrt(ATTN)
    half = CHUNK // 2
    ri = lax.broadcasted_iota(I32, (half, half), 0)
    ci = lax.broadcasted_iota(I32, (half, half), 1)
    allowed = jnp.logical_and(ri // BLOCKS == ci // BLOCKS, ci <= ri)

    for s in range(2):
        def gather(b, _):
            r = s * BLOCKS + b
            for t, (lane0, conds) in enumerate(TAPS):
                upper = {
                    c: tc[pl.ds(gsm[r, COND + lane0 + c] * 8, 8), :]
                    for c in sorted(set(conds))
                }
                for c in range(COLS):
                    x = tb[pl.ds(gsm[r, lane0 + c] * 8, 8), :] + upper[conds[c]]
                    act[t, pl.ds(c * BLOCKS + b, 8, stride=CHUNK), :] = x
            return 0

        lax.fori_loop(0, BLOCKS, gather, 0, unroll=2)

        def pack(i, _):
            for t in range(3):
                for g in range(GROUPS):
                    x = act[t, pl.ds(g * CHUNK + i * 64, 64), :]
                    lhs[pl.ds(i * 64, 64), t * CH + g * 128 : t * CH + (g + 1) * 128] = (
                        jnp.maximum(x, 0.0).astype(BF16)
                    )
            return 0

        lax.fori_loop(0, CHUNK // 64, pack, 0)

        for n in range(CH // 512):
            acc = jnp.dot(
                lhs[...], wconv[:, n * 512 : (n + 1) * 512], preferred_element_type=F32
            )
            hidden[:, n * 512 : (n + 1) * 512] = jnp.maximum(acc, 0.0).astype(BF16)

        for n in range(CH // 512):
            acc = jnp.dot(
                hidden[...], wmix[:, n * 512 : (n + 1) * 512], preferred_element_type=F32
            )
            for g in range(4):
                stream = act[1, pl.ds((4 * n + g) * CHUNK, CHUNK), :]
                resid[:, n * 512 + g * 128 : n * 512 + (g + 1) * 128] = (
                    stream + acc[:, g * 128 : (g + 1) * 128]
                ).astype(BF16)

        for n0, n1 in ((0, 512), (512, 1024), (1024, 1536), (1536, WIDTH)):
            pj[:, n0:n1] = jnp.dot(resid[...], wproj[:, n0:n1], preferred_element_type=F32)

        def norm(i, _):
            x = pj[pl.ds(i * 64, 64), :]
            x = x - jnp.mean(x, axis=-1, keepdims=True)
            var = jnp.mean(x * x, axis=-1, keepdims=True)
            y = x / jnp.sqrt(var + 1e-05) * gain_ref[...] + bias_ref[...]
            normed[pl.ds(i * 64, 64), :] = y.astype(BF16)
            return 0

        lax.fori_loop(0, CHUNK // 64, norm, 0)

        for n in range(3):
            qkv[n] = lax.dot_general(
                normed[...],
                wattn[n * ATTN : (n + 1) * ATTN, :],
                (((1,), (1,)), ((), ())),
                preferred_element_type=F32,
            ).astype(BF16)

        for p in range(2):
            rows = slice(p * half, (p + 1) * half)
            query = qkv[0, rows, :]
            keys = qkv[1, rows, :]
            values = qkv[2, rows, :]
            scores = lax.dot_general(
                query, keys, (((1,), (1,)), ((), ())), preferred_element_type=F32
            ) * scale
            scores = jnp.where(allowed, scores, -jnp.inf)
            e = jnp.exp(scores - jnp.max(scores, axis=-1, keepdims=True))
            w = (e / jnp.sum(e, axis=-1, keepdims=True)).astype(BF16)
            mixed = jnp.dot(w, values, preferred_element_type=F32)
            for g in range(4):
                wide = min(128, ATTN - g * 128)
                att[g, rows, 0:wide] = mixed[:, g * 128 : g * 128 + wide]

        def regroup(i, _):
            for v in range(2):
                for g in range(4):
                    x = att[g, pl.ds(2 * i + v, COLS, stride=BLOCKS), :]
                    wide = min(128, ATTN - g * 128)
                    sendo[s, i, v * COLS : (v + 1) * COLS, g * 128 : g * 128 + wide] = x[
                        :, :wide
                    ].astype(BF16)
            return 0

        lax.fori_loop(0, SEQ, regroup, 0, unroll=2)

        song = 2 * h + s

        def send_out(t, _):
            peer = lax.rem(j + t, SEQ)
            pltpu.make_async_remote_copy(
                src_ref=sendo.at[s, peer],
                dst_ref=out_ref.at[song, k],
                send_sem=osend_sem.at[s],
                recv_sem=orecv_sem.at[s],
                device_id=(a, peer),
                device_id_type=MESH,
            ).start()
            return 0

        lax.fori_loop(1, SEQ, send_out, 0)
        pltpu.make_async_copy(sendo.at[s, j], out_ref.at[song, k], local_sem.at[s]).start()

    for s in range(2):
        view = sendo.at[s, pl.ds(0, SEQ - 1)]
        pltpu.make_async_copy(view, view, osend_sem.at[s]).wait()
        pltpu.make_async_copy(view, view, orecv_sem.at[s]).wait()
        pltpu.make_async_copy(sendo.at[s, j], out_ref.at[2 * h + s, k], local_sem.at[s]).wait()
    code_wait(SEQ - 1, csend_sem)

    @pl.when(jnp.logical_or(to_next, to_prev))
    def _():
        code_wait(SEQ, csend_sem)


def body(
    bottom_codes, cond_codes, bottom_table, cond_table, conv_dilated, conv_mix,
    projection, norm_gain, norm_bias, attn_weight,
):
    vmem = pl.BlockSpec(memory_space=pltpu.VMEM)
    hbm = pl.BlockSpec(memory_space=pl.ANY)
    dma = pltpu.SemaphoreType.DMA
    out = pl.pallas_call(
        kernel,
        out_shape=jax.ShapeDtypeStruct((4, SEQ // 2, 16, ATTN), BF16),
        in_specs=[vmem] * 4 + [hbm] * 6,
        out_specs=hbm,
        scratch_shapes=[
            pltpu.VMEM((VOCAB * 8 + 8, 128), F32),
            pltpu.VMEM((VOCAB * 8, 128), F32),
            pltpu.VMEM((4, STAGE, CH), BF16),
            pltpu.VMEM((3 * CH, CH), BF16),
            pltpu.VMEM((CH, CH), BF16),
            pltpu.VMEM((CH, WIDTH), BF16),
            pltpu.VMEM((3 * ATTN, WIDTH), BF16),
            pltpu.VMEM((2, 8, 128), I32),
            pltpu.VMEM((SLOTS, 8, 128), I32),
            pltpu.VMEM((2 * BLOCKS, 128), I32),
            pltpu.SMEM((2 * BLOCKS, 128), I32),
            pltpu.VMEM((3, GROUPS * CHUNK, 128), F32),
            pltpu.VMEM((CHUNK, 3 * CH), BF16),
            pltpu.VMEM((CHUNK, CH), BF16),
            pltpu.VMEM((CHUNK, CH), BF16),
            pltpu.VMEM((CHUNK, WIDTH), F32),
            pltpu.VMEM((CHUNK, WIDTH), BF16),
            pltpu.VMEM((3, CHUNK, ATTN), BF16),
            pltpu.VMEM((4, CHUNK, 128), F32),
            pltpu.VMEM((2, SEQ, 16, ATTN), BF16),
            dma((4,)),
            dma((4,)),
            dma,
            dma((3,)),
            dma,
            dma((2,)),
            dma((2,)),
            dma((2,)),
        ],
        compiler_params=pltpu.CompilerParams(
            collective_id=0, has_side_effects=True, vmem_limit_bytes=63 * 1024 * 1024
        ),
        cost_estimate=pl.CostEstimate(
            flops=18_300_000_000, bytes_accessed=28_000_000, transcendentals=300_000
        ),
        name="upsampler",
    )(
        bottom_codes, cond_codes, norm_gain.reshape(1, WIDTH), norm_bias.reshape(1, WIDTH),
        bottom_table, cond_table, conv_dilated.reshape(3 * CH, CH), conv_mix, projection,
        attn_weight.T,
    )
    songs = bottom_codes.shape[0]
    out = out.reshape(songs, SEQ // 2, 2, COLS, ATTN).transpose(0, 2, 1, 3, 4)
    return out.reshape(songs, ROWS, ATTN)


def solution(mesh):
    split = P(None, ("ctx", "seq"))
    return jax.shard_map(
        body,
        mesh=mesh,
        in_specs=(split, split) + (P(),) * 8,
        out_specs=P(None, ("ctx", "seq"), None),
        check_vma=False,
    )
```

profile of v0, /device:TPU:1, one launch (start us, length us, event | category | flops | bytes accessed | tf_op | source)
XLA Modules:
  0.0 75.9 jit_solution(3877953548185564789)
XLA Ops:
  0.0 1.3 %reshape.15.gain_ref = f32[1,1920]{1,0:T(1,128)} reshape(f32[1920]{0:T(1024)} %param.17) | data formatting | bytes 15360 | tf_op jit(solution)/shard_map/reshape | solution.py:406
  1.3 1.3 %reshape.16.bias_ref = f32[1,1920]{1,0:T(1,128)} reshape(f32[1920]{0:T(1024)} %param.18) | data formatting | bytes 15360 | tf_op jit(solution)/shard_map/reshape | solution.py:406
  2.6 70.7 %upsampler.1 = bf16[4,16,16,480]{3,2,1,0:T(8,128)(2,1)} custom-call(s32[4,256]{1,0:T(4,128)} %bottom_ref.1, s32[4,64]{1,0:T(4,128)} %cond_ref.1, f32[1,1920]{1,0:T(1,128)} %reshape.15.gain_ref, f32[1,1920]{1,0:T(1,128)} %reshape.16.bias_ref, bf16[2048,1024]{1,0:T(8,128)(2,1)} %btab.1, bf16[2048,1024]{1,0:T(8,128)(2,1)} %ctab.1, bf16[3072,1024]{1,0:T(8,128)(2,1)} %bitcast.8, ...), custom_call_target="tpu_custom_call" | custom-call | flops 18300000256 | bytes 28000000 | tf_op jit(solution)/shard_map/upsampler/pallas_call | solution.py:363
  73.3 1.3 %copy.12 = bf16[4,16,2,8,480]{4,3,1,2,0:T(8,128)(2,1)S(1)} copy(bf16[4,16,2,8,480]{4,3,2,1,0:T(8,128)(2,1)} %bitcast.7) | data formatting | bytes 1966080 | tf_op jit(solution)/shard_map/reshape | solution.py:411
  74.6 1.3 %copy.13 = bf16[4,256,480]{1,2,0:T(8,128)(2,1)} copy(bf16[4,256,480]{2,1,0:T(8,128)(2,1)S(1)} %bitcast.6) | data formatting | bytes 1966080 | tf_op jit(solution)/shard_map/reshape | solution.py:412
where the time goes:
time: 76.2 us; the launch traced here: 75.9 us
  Pallas kernels  70.7 us (93%)
  local copies, waits for them, and re-layouts  5.2 us (7%)
    pallas_call x1, Pallas kernels, body(): pl.pallas_call(kernel, out_shape=jax.ShapeDtypeStruct((4, SEQ // 2, 16, A...  70.7 us

commit v1 on v0

--- a/solution.py
+++ b/solution.py
@@ -22,6 +22,8 @@
 CHUNK = BLOCKS * COLS
 VOCAB, CH, WIDTH, ATTN = 2048, 1024, 1920, 480
 GROUPS = CH // 128
+PITCH = CHUNK + 8
+CPITCH = BLOCKS + 8
 NOWHERE = VOCAB * 8
 STAGE = 512
 OWN, LEFT, RIGHT = 0, 8, 16
@@ -224,34 +226,31 @@
     to_smem.start()
     to_smem.wait()
 
-    for w in weights:
-        w.wait()
-
     scale = 1.0 / math.sqrt(ATTN)
     half = CHUNK // 2
     ri = lax.broadcasted_iota(I32, (half, half), 0)
     ci = lax.broadcasted_iota(I32, (half, half), 1)
     allowed = jnp.logical_and(ri // BLOCKS == ci // BLOCKS, ci <= ri)
 
-    for s in range(2):
+    def gather_rows(s):
         def gather(b, _):
             r = s * BLOCKS + b
             for t, (lane0, conds) in enumerate(TAPS):
-                upper = {
-                    c: tc[pl.ds(gsm[r, COND + lane0 + c] * 8, 8), :]
-                    for c in sorted(set(conds))
-                }
+                upper = [
+                    tc[pl.ds(gsm[r, COND + lane0 + c] * 8, 8), :] for c in range(max(conds) + 1)
+                ]
                 for c in range(COLS):
                     x = tb[pl.ds(gsm[r, lane0 + c] * 8, 8), :] + upper[conds[c]]
-                    act[t, pl.ds(c * BLOCKS + b, 8, stride=CHUNK), :] = x
+                    act[t, pl.ds(c * BLOCKS + b, 8, stride=PITCH), :] = x
             return 0
 
         lax.fori_loop(0, BLOCKS, gather, 0, unroll=2)
 
+    def pack_rows(s):
         def pack(i, _):
             for t in range(3):
                 for g in range(GROUPS):
-                    x = act[t, pl.ds(g * CHUNK + i * 64, 64), :]
+                    x = act[t, pl.ds(g * PITCH + i * 64, 64), :]
                     lhs[pl.ds(i * 64, 64), t * CH + g * 128 : t * CH + (g + 1) * 128] = (
                         jnp.maximum(x, 0.0).astype(BF16)
                     )
@@ -259,35 +258,50 @@
 
         lax.fori_loop(0, CHUNK // 64, pack, 0)
 
+    def ready(s, i):
+        if s == 0:
+            weights[i].wait()
+
+    def convolve(s):
+        ready(s, 0)
         for n in range(CH // 512):
             acc = jnp.dot(
                 lhs[...], wconv[:, n * 512 : (n + 1) * 512], preferred_element_type=F32
             )
             hidden[:, n * 512 : (n + 1) * 512] = jnp.maximum(acc, 0.0).astype(BF16)
 
+    def mix_rows(s):
+        ready(s, 1)
         for n in range(CH // 512):
             acc = jnp.dot(
                 hidden[...], wmix[:, n * 512 : (n + 1) * 512], preferred_element_type=F32
             )
             for g in range(4):
-                stream = act[1, pl.ds((4 * n + g) * CHUNK, CHUNK), :]
+                stream = act[1, pl.ds((4 * n + g) * PITCH, CHUNK), :]
                 resid[:, n * 512 + g * 128 : n * 512 + (g + 1) * 128] = (
                     stream + acc[:, g * 128 : (g + 1) * 128]
                 ).astype(BF16)
 
+    def project(s):
+        ready(s, 2)
         for n0, n1 in ((0, 512), (512, 1024), (1024, 1536), (1536, WIDTH)):
             pj[:, n0:n1] = jnp.dot(resid[...], wproj[:, n0:n1], preferred_element_type=F32)
 
+    def normalise(s):
         def norm(i, _):
             x = pj[pl.ds(i * 64, 64), :]
             x = x - jnp.mean(x, axis=-1, keepdims=True)
             var = jnp.mean(x * x, axis=-1, keepdims=True)
-            y = x / jnp.sqrt(var + 1e-05) * gain_ref[...] + bias_ref[...]
-            normed[pl.ds(i * 64, 64), :] = y.astype(BF16)
+            x = x * lax.rsqrt(var + 1e-05)
+            for g in range(WIDTH // 128):
+                y = x[:, g * 128 : (g + 1) * 128] * gain_ref[g : g + 1, :] + bias_ref[g : g + 1, :]
+                normed[pl.ds(i * 64, 64), g * 128 : (g + 1) * 128] = y.astype(BF16)
             return 0
 
         lax.fori_loop(0, CHUNK // 64, norm, 0)
 
+    def make_qkv(s):
+        ready(s, 3)
         for n in range(3):
             qkv[n] = lax.dot_general(
                 normed[...],
@@ -296,6 +310,7 @@
                 preferred_element_type=F32,
             ).astype(BF16)
 
+    def attend(s):
         for p in range(2):
             rows = slice(p * half, (p + 1) * half)
             query = qkv[0, rows, :]
@@ -306,16 +321,20 @@
             ) * scale
             scores = jnp.where(allowed, scores, -jnp.inf)
             e = jnp.exp(scores - jnp.max(scores, axis=-1, keepdims=True))
-            w = (e / jnp.sum(e, axis=-1, keepdims=True)).astype(BF16)
+            w = (e * (1.0 / jnp.sum(e, axis=-1, keepdims=True))).astype(BF16)
             mixed = jnp.dot(w, values, preferred_element_type=F32)
             for g in range(4):
                 wide = min(128, ATTN - g * 128)
-                att[g, rows, 0:wide] = mixed[:, g * 128 : g * 128 + wide]
-
+                for c in range(COLS // 2):
+                    att[g, pl.ds((p * COLS // 2 + c) * CPITCH, BLOCKS), 0:wide] = mixed[
+                        c * BLOCKS : (c + 1) * BLOCKS, g * 128 : g * 128 + wide
+                    ]
+
+    def regroup_rows(s):
         def regroup(i, _):
             for v in range(2):
                 for g in range(4):
-                    x = att[g, pl.ds(2 * i + v, COLS, stride=BLOCKS), :]
+                    x = att[g, pl.ds(2 * i + v, COLS, stride=CPITCH), :]
                     wide = min(128, ATTN - g * 128)
                     sendo[s, i, v * COLS : (v + 1) * COLS, g * 128 : g * 128 + wide] = x[
                         :, :wide
@@ -324,6 +343,7 @@
 
         lax.fori_loop(0, SEQ, regroup, 0, unroll=2)
 
+    def send_rows(s):
         song = 2 * h + s
 
         def send_out(t, _):
@@ -340,6 +360,18 @@
 
         lax.fori_loop(1, SEQ, send_out, 0)
         pltpu.make_async_copy(sendo.at[s, j], out_ref.at[song, k], local_sem.at[s]).start()
+
+    for s in range(2):
+        gather_rows(s)
+        pack_rows(s)
+        convolve(s)
+        mix_rows(s)
+        project(s)
+        normalise(s)
+        make_qkv(s)
+        attend(s)
+        regroup_rows(s)
+        send_rows(s)
 
     for s in range(2):
         view = sendo.at[s, pl.ds(0, SEQ - 1)]
@@ -377,14 +409,14 @@
             pltpu.VMEM((SLOTS, 8, 128), I32),
             pltpu.VMEM((2 * BLOCKS, 128), I32),
             pltpu.SMEM((2 * BLOCKS, 128), I32),
-            pltpu.VMEM((3, GROUPS * CHUNK, 128), F32),
+            pltpu.VMEM((3, GROUPS * PITCH, 128), F32),
             pltpu.VMEM((CHUNK, 3 * CH), BF16),
             pltpu.VMEM((CHUNK, CH), BF16),
             pltpu.VMEM((CHUNK, CH), BF16),
             pltpu.VMEM((CHUNK, WIDTH), F32),
             pltpu.VMEM((CHUNK, WIDTH), BF16),
             pltpu.VMEM((3, CHUNK, ATTN), BF16),
-            pltpu.VMEM((4, CHUNK, 128), F32),
+            pltpu.VMEM((4, COLS * CPITCH, 128), F32),
             pltpu.VMEM((2, SEQ, 16, ATTN), BF16),
             dma((4,)),
             dma((4,)),
@@ -403,7 +435,8 @@
         ),
         name="upsampler",
     )(
-        bottom_codes, cond_codes, norm_gain.reshape(1, WIDTH), norm_bias.reshape(1, WIDTH),
+        bottom_codes, cond_codes, norm_gain.reshape(WIDTH // 128, 128),
+        norm_bias.reshape(WIDTH // 128, 128),
         bottom_table, cond_table, conv_dilated.reshape(3 * CH, CH), conv_mix, projection,
         attn_weight.T,
     )

time: 76.2 us -> 63.7 us (0.84)
  Pallas kernels: 70.7 us -> 60.9 us
  local copies, waits for them, and re-layouts: 5.2 us -> 2.61 us
    pallas_call x1, Pallas kernels: 70.7 us -> 60.9 us  [body(): pl.pallas_call(kernel, out_shape=jax.ShapeDtypeStruct((4, SEQ // 2, 16, A...]
    reshape x2 -> x0, local copies, waits for them, and re-layouts: 2.59 us -> none  [the longest x1 1.3 us: body(): norm_gain.reshape(1, WIDTH)]
where the time goes in v1:
time: 63.7 us; the launch traced here: 63.5 us
  Pallas kernels  60.9 us (96%)
  local copies, waits for them, and re-layouts  2.61 us (4%)
    pallas_call x1, Pallas kernels, body(): pl.pallas_call(kernel, out_shape=jax.ShapeDtypeStruct((4, SEQ // 2, 16, A...  60.9 us
    reshape x1, local copies, waits for them, and re-layouts, body(): out = out.reshape(songs, SEQ // 2, 2, COLS, ATTN).transpose(0, 2, 1, 3, 4)  1.32 us
    reshape x1, local copies, waits for them, and re-layouts, body(): return out.reshape(songs, ROWS, ATTN)  1.29 us

profile of v1, /device:TPU:1, one launch (start us, length us, event | category | flops | bytes accessed | tf_op | source)
XLA Modules:
  0.0 63.5 jit_solution(5859144462757244516)
XLA Ops:
  0.0 60.9 %upsampler.1 = bf16[4,16,16,480]{3,2,1,0:T(8,128)(2,1)} custom-call(s32[4,256]{1,0:T(4,128)} %bottom_ref.1, s32[4,64]{1,0:T(4,128)} %cond_ref.1, f32[15,128]{1,0:T(8,128)} %bitcast.12, f32[15,128]{1,0:T(8,128)} %bitcast.13, bf16[2048,1024]{1,0:T(8,128)(2,1)} %btab.1, bf16[2048,1024]{1,0:T(8,128)(2,1)} %ctab.1, bf16[3072,1024]{1,0:T(8,128)(2,1)} %bitcast.10, ...), custom_call_target="tpu_custom_call" | custom-call | flops 18300000256 | bytes 28000000 | tf_op jit(solution)/shard_map/upsampler/pallas_call | solution.py:395
  60.9 1.3 %copy.12 = bf16[4,16,2,8,480]{4,3,1,2,0:T(8,128)(2,1)S(1)} copy(bf16[4,16,2,8,480]{4,3,2,1,0:T(8,128)(2,1)} %bitcast.9) | data formatting | bytes 1966080 | tf_op jit(solution)/shard_map/reshape | solution.py:444
  62.2 1.3 %copy.13 = bf16[4,256,480]{1,2,0:T(8,128)(2,1)} copy(bf16[4,256,480]{2,1,0:T(8,128)(2,1)S(1)} %bitcast.8) | data formatting | bytes 1966080 | tf_op jit(solution)/shard_map/reshape | solution.py:445

commit v2 on v0

v2 whole, which is shorter than its diff:
```python
import functools
import math

import jax
import jax.numpy as jnp
from jax import lax
from jax.experimental import pallas as pl
from jax.experimental.pallas import tpu as pltpu
from jax.sharding import PartitionSpec as P

F32, BF16, I32 = jnp.float32, jnp.bfloat16, jnp.int32
MESH = pl.DeviceIdType.MESH

BLOCK = 128
DIL_BLOCKS, DIL_REST = divmod(2187, BLOCK)
CTX, SEQ = 4, 32
ROWS = 256
HALO = 9
SLOTS = SEQ + 2 * HALO
BLOCKS = 64
COLS = 4
CHUNK = BLOCKS * COLS
HALF = CHUNK // 2
CHUNKS = 4
VOCAB, CH, WIDTH, ATTN = 2048, 1024, 1920, 480
GROUPS = CH // 128
PITCH = CHUNK + 8
CPITCH = SEQ + 8
NOWHERE = VOCAB * 8
STAGE = 512
OWN, LEFT, RIGHT = 0, 8, 16
COND = 32
TAPS = ((LEFT, (0, 0, 0, 1)), (OWN, (0, 0, 0, 0)), (RIGHT, (0, 1, 1, 1)))


def kernel(
    bottom_ref, cond_ref, gain_ref, bias_ref, btab, ctab, conv, mix, proj, attn,
    out_ref,
    tb, tc, stage, wconv, wmix, wproj, wattn,
    sendc, codes, gath, gsm,
    stream, act, lhs, hidden, resid, pj, normed, qkv, att, sendo, got, turned,
    stage_sem, w_sem, csend_sem, crecv_sem, g_sem, osend_sem, orecv_sem, local_sem, out_sem,
):
    a = lax.axis_index("ctx")
    j = lax.axis_index("seq")
    k = j // 2
    h = j % 2

    to_next = jnp.logical_and(a < CTX - 1, j >= SEQ - HALO)
    to_prev = jnp.logical_and(a > 0, j < HALO)

    barrier = pltpu.get_barrier_semaphore()

    def greet(t, _):
        pl.semaphore_signal(
            barrier, inc=1, device_id=(a, lax.rem(j + t, SEQ)), device_id_type=MESH
        )
        return 0

    lax.fori_loop(1, SEQ, greet, 0)

    @pl.when(a > 0)
    def _():
        def f(t, _):
            pl.semaphore_signal(barrier, inc=1, device_id=(a - 1, t), device_id_type=MESH)
            return 0

        lax.fori_loop(SEQ - HALO, SEQ, f, 0)

    @pl.when(a < CTX - 1)
    def _():
        def f(t, _):
            pl.semaphore_signal(barrier, inc=1, device_id=(a + 1, t), device_id_type=MESH)
            return 0

        lax.fori_loop(0, HALO, f, 0)

    def stage_copy(i):
        table = (btab, ctab)[i // 4]
        return pltpu.make_async_copy(
            table.at[pl.ds((i % 4) * STAGE, STAGE)], stage.at[i % 4], stage_sem.at[i % 4]
        )

    weights = [
        pltpu.make_async_copy(src, dst, w_sem.at[i])
        for i, (src, dst) in enumerate(
            ((conv, wconv), (mix, wmix), (proj, wproj), (attn, wattn))
        )
    ]
    for i in range(4):
        stage_copy(i).start()

    sendc[...] = jnp.zeros_like(sendc)
    for song in range(4):
        p, s = divmod(song, 2)
        for u in range(2):
            sendc[p, 2 * s + u : 2 * s + u + 1, :] = bottom_ref[
                song : song + 1, u * 128 : (u + 1) * 128
            ]
            sendc[p, 4 + s : 5 + s, u * 64 : (u + 1) * 64] = cond_ref[song : song + 1, :]

    def widen(i):
        table = (tb, tc)[i // 4]
        stage_copy(i).wait()

        def f(r, _):
            x = stage[i % 4, pl.ds(r * 16, 16), :].astype(F32)
            base = ((i % 4) * STAGE + r * 16) * 8
            for q in range(2):
                for g in range(GROUPS):
                    table[pl.ds(base + q * 64 + g, 8, stride=8), :] = x[
                        8 * q : 8 * q + 8, 128 * g : 128 * g + 128
                    ]
            return 0

        lax.fori_loop(0, STAGE // 16, f, 0, unroll=2)
        if i + 4 < 8:
            stage_copy(i + 4).start()

    for i in range(2):
        widen(i)

    pl.semaphore_wait(barrier, SEQ - 1 + jnp.where(jnp.logical_or(to_next, to_prev), SEQ, 0))

    def send_codes(ctx, peer, slot, sem):
        pltpu.make_async_remote_copy(
            src_ref=sendc.at[peer % 2],
            dst_ref=codes.at[slot],
            send_sem=csend_sem,
            recv_sem=crecv_sem.at[sem],
            device_id=(ctx, peer),
            device_id_type=MESH,
        ).start()

    def own_codes(t, _):
        send_codes(a, lax.rem(j + t, SEQ), j + HALO, 0)
        return 0

    lax.fori_loop(1, SEQ, own_codes, 0)

    @pl.when(to_next)
    def _():
        def f(t, _):
            send_codes(a + 1, t, j - (SEQ - HALO), 1)
            return 0

        lax.fori_loop(0, SEQ, f, 0)

    @pl.when(to_prev)
    def _():
        def f(t, _):
            send_codes(a - 1, t, j + SEQ + HALO, 2)
            return 0

        lax.fori_loop(0, SEQ, f, 0)

    codes[j + HALO] = sendc[h]
    outside = jnp.where(lax.broadcasted_iota(I32, (HALO, 8, 128), 1) < 4, VOCAB, 0)

    @pl.when(a == 0)
    def _():
        codes[0:HALO] = outside

    @pl.when(a == CTX - 1)
    def _():
        codes[SEQ + HALO : SLOTS] = outside

    for i in range(2, 4):
        widen(i)
    for w in weights:
        w.start()
    tb[pl.ds(NOWHERE, 8), :] = jnp.full((8, 128), -1e9, F32)

    for i in range(4, 8):
        widen(i)

    def code_wait(count, sem):
        view = codes.at[pl.ds(0, count)]
        pltpu.make_async_copy(view, view, sem).wait()

    code_wait(SEQ - 1, crecv_sem.at[0])

    @pl.when(a > 0)
    def _():
        code_wait(HALO, crecv_sem.at[1])

    @pl.when(a < CTX - 1)
    def _():
        code_wait(HALO, crecv_sem.at[2])

    lanes = lax.broadcasted_iota(I32, (BLOCKS // 2, 128), 1)

    def to_smem(s):
        rows = pl.ds(s * SEQ, SEQ)
        return pltpu.make_async_copy(gath.at[rows], gsm.at[rows], g_sem.at[s])

    for s in range(2):
        pair = None
        for v in range(2):
            def bottom(beta):
                d, u = divmod(beta, 2)
                return codes[d : d + BLOCKS // 2, 2 * s + u, :]

            def upper(beta):
                d, u = divmod(beta, 2)
                x = codes[d : d + BLOCKS // 2, 4 + s, :]
                if u:
                    y = codes[d + 1 : d + 1 + BLOCKS // 2, 4 + s, :]
                    x = jnp.where(lanes < 64, x, y)
                return x, 32 * u

            lead = v + 2 * HALO
            before, after = lead - DIL_BLOCKS, lead + DIL_BLOCKS
            left = jnp.where(lanes >= 128 - DIL_REST, bottom(before - 1), bottom(before))
            right = jnp.where(lanes < DIL_REST, bottom(after + 1), bottom(after))
            up_own, own0 = upper(lead)
            up_left, left0 = upper(before - 1)
            up_right, right0 = upper(after)
            row = None
            for x, lane0, first, step in (
                (bottom(lead), OWN, 0, 8),
                (left, LEFT, -DIL_REST, 8),
                (right, RIGHT, DIL_REST, 8),
                (up_own, COND + OWN, own0, 2),
                (up_left, COND + LEFT, left0 + 32 - 3, 2),
                (up_right, COND + RIGHT, right0 + 2, 2),
            ):
                lane0 += 64 * v
                amount = lax.rem(lane0 - first + 256 - step * k, 128)
                rolled = pltpu.roll(x, amount, 1)
                row = rolled if row is None else jnp.where(lanes >= lane0, rolled, row)
            pair = row if pair is None else jnp.where(lanes < 64, pair, row)
        gath[s * SEQ : (s + 1) * SEQ, :] = pair * 8
        to_smem(s).start()
    to_smem(0).wait()

    scale = 1.0 / math.sqrt(ATTN)
    ri = lax.broadcasted_iota(I32, (CHUNK, CHUNK), 0)
    ci = lax.broadcasted_iota(I32, (CHUNK, CHUNK), 1)
    allowed = jnp.logical_and(
        (ri // SEQ) % COLS == (ci // SEQ) % COLS,
        2 * (ci % SEQ) + ci // HALF <= 2 * (ri % SEQ) + ri // HALF,
    )

    def gather_rows(i, first, count):
        s, p = divmod(i, 2)
        for q in range(count):
            b = first + q
            r, at = s * SEQ + b // 2, (q % 2) * 64
            row = b // 2 + (q % 2) * HALF
            for t, (lane0, conds) in enumerate(TAPS):
                upper = [
                    tc[pl.ds(gsm[r, at + COND + lane0 + p + c], 8), :]
                    for c in range(max(conds) + 1)
                ]
                for c in range(COLS):
                    x = tb[pl.ds(gsm[r, at + lane0 + COLS * p + c], 8), :] + upper[conds[c]]
                    if t == 1:
                        stream[i % 2, pl.ds(row + c * SEQ, 8, stride=PITCH), :] = x
                    else:
                        act[t // 2, pl.ds(row + c * SEQ, 8, stride=PITCH), :] = x

    def pack_rows(i, first, count):
        for t in range(3):
            for g in range(GROUPS):
                rows = pl.ds(g * PITCH + first, count)
                x = stream[i % 2, rows, :] if t == 1 else act[t // 2, rows, :]
                lhs[first : first + count, t * CH + g * 128 : t * CH + (g + 1) * 128] = (
                    jnp.maximum(x, 0.0).astype(BF16)
                )

    def convolve(i, n):
        cols = slice(n * 256, (n + 1) * 256)
        acc = jnp.dot(lhs[...], wconv[:, cols], preferred_element_type=F32)
        hidden[:, cols] = jnp.maximum(acc, 0.0).astype(BF16)

    def mix_rows(i):
        for n in range(CH // 256):
            acc = jnp.dot(
                hidden[...], wmix[:, n * 256 : (n + 1) * 256], preferred_element_type=F32
            )
            for g in range(2):
                own = stream[i % 2, pl.ds((2 * n + g) * PITCH, CHUNK), :]
                resid[:, n * 256 + g * 128 : n * 256 + (g + 1) * 128] = (
                    own + acc[:, g * 128 : (g + 1) * 128]
                ).astype(BF16)

    def project(n0, n1):
        pj[:, n0:n1] = jnp.dot(resid[...], wproj[:, n0:n1], preferred_element_type=F32)

    def normalise(first, count):
        rows = slice(first, first + count)
        x = pj[rows, :]
        x = x - jnp.mean(x, axis=-1, keepdims=True)
        var = jnp.mean(x * x, axis=-1, keepdims=True)
        x = x * lax.rsqrt(var + 1e-05)
        for g in range(WIDTH // 128):
            y = x[:, g * 128 : (g + 1) * 128] * gain_ref[g : g + 1, :] + bias_ref[g : g + 1, :]
            normed[rows, g * 128 : (g + 1) * 128] = y.astype(BF16)

    def make_qkv(n):
        qkv[n] = lax.dot_general(
            normed[...],
            wattn[n * ATTN : (n + 1) * ATTN, :],
            (((1,), (1,)), ((), ())),
            preferred_element_type=F32,
        ).astype(BF16)

    def attend():
        scores = lax.dot_general(
            qkv[0], qkv[1], (((1,), (1,)), ((), ())), preferred_element_type=F32
        ) * scale
        scores = jnp.where(allowed, scores, -jnp.inf)
        e = jnp.exp(scores - jnp.max(scores, axis=-1, keepdims=True))
        w = (e * (1.0 / jnp.sum(e, axis=-1, keepdims=True))).astype(BF16)
        mixed = jnp.dot(w, qkv[2], preferred_element_type=F32)
        for g in range(4):
            wide = min(128, ATTN - g * 128)
            for c in range(8):
                att[g, c * CPITCH : c * CPITCH + SEQ, 0:wide] = mixed[
                    c * SEQ : (c + 1) * SEQ, g * 128 : g * 128 + wide
                ]

    def regroup_rows(i):
        def regroup(d, _):
            for g in range(4):
                x = att[g, pl.ds(d, 8, stride=CPITCH), :]
                wide = min(128, ATTN - g * 128)
                sendo[i, d, :, g * 128 : g * 128 + wide] = x[:, :wide].astype(BF16)
            return 0

        lax.fori_loop(0, SEQ, regroup, 0, unroll=8)

    def send_rows(i):
        s, p = divmod(i, 2)
        song = 2 * h + s

        def send_out(t, _):
            peer = lax.rem(j + t, SEQ)
            pltpu.make_async_remote_copy(
                src_ref=sendo.at[i, peer],
                dst_ref=got.at[song, k, p],
                send_sem=osend_sem.at[i],
                recv_sem=orecv_sem.at[i],
                device_id=(a, peer),
                device_id_type=MESH,
            ).start()
            return 0

        lax.fori_loop(1, SEQ, send_out, 0)
        pltpu.make_async_copy(sendo.at[i, j], got.at[song, k, p], local_sem.at[i]).start()

    def first_rows(e, _):
        gather_rows(0, e * 4, 4)
        return 0

    lax.fori_loop(0, BLOCKS // 4, first_rows, 0)
    for q in range(4):
        pack_rows(0, q * 64, 64)

    for i in range(CHUNKS):
        if i == 0:
            weights[0].wait()

        for n in range(CH // 256):
            convolve(i, n)
            if i + 1 < CHUNKS:
                gather_rows(i + 1, n * 16, 16)
        if i == 0:
            weights[1].wait()
        mix_rows(i)
        if i == 0:
            weights[2].wait()
        for q, (n0, n1) in enumerate(((0, 512), (512, 1024), (1024, 1536), (1536, WIDTH))):
            project(n0, n1)
            if i + 1 < CHUNKS:
                pack_rows(i + 1, q * 64, 64)
        normalise(0, CHUNK)
        if i == 0:
            weights[3].wait()
            to_smem(1).wait()
        for n in range(3):
            make_qkv(n)
        attend()
        regroup_rows(i)
        send_rows(i)

    ri = lax.broadcasted_iota(I32, (ROWS, ROWS), 0)
    ci = lax.broadcasted_iota(I32, (ROWS, ROWS), 1)
    place = (ri // 8) * COLS + ri % COLS + ((ri // COLS) % 2) * BLOCK
    order = jnp.where(place == ci, 1.0, 0.0).astype(BF16)
    out_copies = []
    for s in range(2):
        for i in (2 * s, 2 * s + 1):
            view = sendo.at[i, pl.ds(0, SEQ - 1)]
            pltpu.make_async_copy(view, view, osend_sem.at[i]).wait()
            pltpu.make_async_copy(view, view, orecv_sem.at[i]).wait()
            pltpu.make_async_copy(
                sendo.at[i, j], got.at[2 * h + s, k, i % 2], local_sem.at[i]
            ).wait()
        for song in (s, s + 2):
            x = got[song].astype(F32).reshape(ROWS, ATTN).astype(BF16)
            turned[song] = lax.dot_general(
                x, order, (((0,), (0,)), ((), ())), preferred_element_type=F32
            ).astype(BF16)
            copy = pltpu.make_async_copy(turned.at[song], out_ref.at[song], out_sem.at[song])
            copy.start()
            out_copies.append(copy)
    for copy in out_copies:
        copy.wait()
    code_wait(SEQ - 1, csend_sem)

    @pl.when(jnp.logical_or(to_next, to_prev))
    def _():
        code_wait(SEQ, csend_sem)


def body(
    bottom_codes, cond_codes, bottom_table, cond_table, conv_dilated, conv_mix,
    projection, norm_gain, norm_bias, attn_weight,
):
    vmem = pl.BlockSpec(memory_space=pltpu.VMEM)
    hbm = pl.BlockSpec(memory_space=pl.ANY)
    dma = pltpu.SemaphoreType.DMA
    out = pl.pallas_call(
        kernel,
        out_shape=jax.ShapeDtypeStruct((4, ATTN, ROWS), BF16),
        in_specs=[vmem] * 4 + [hbm] * 6,
        out_specs=hbm,
        scratch_shapes=[
            pltpu.VMEM((VOCAB * 8 + 8, 128), F32),
            pltpu.VMEM((VOCAB * 8, 128), F32),
            pltpu.VMEM((4, STAGE, CH), BF16),
            pltpu.VMEM((3 * CH, CH), BF16),
            pltpu.VMEM((CH, CH), BF16),
            pltpu.VMEM((CH, WIDTH), BF16),
            pltpu.VMEM((3 * ATTN, WIDTH), BF16),
            pltpu.VMEM((2, 8, 128), I32),
            pltpu.VMEM((SLOTS, 8, 128), I32),
            pltpu.VMEM((BLOCKS, 128), I32),
            pltpu.SMEM((BLOCKS, 128), I32),
            pltpu.VMEM((2, GROUPS * PITCH, 128), F32),
            pltpu.VMEM((2, GROUPS * PITCH, 128), F32),
            pltpu.VMEM((CHUNK, 3 * CH), BF16),
            pltpu.VMEM((CHUNK, CH), BF16),
            pltpu.VMEM((CHUNK, CH), BF16),
            pltpu.VMEM((CHUNK, WIDTH), F32),
            pltpu.VMEM((CHUNK, WIDTH), BF16),
            pltpu.VMEM((3, CHUNK, ATTN), BF16),
            pltpu.VMEM((4, 8 * CPITCH, 128), F32),
            pltpu.VMEM((CHUNKS, SEQ, 8, ATTN), BF16),
            pltpu.VMEM((4, SEQ // 2, 2, 8, ATTN), BF16),
            pltpu.VMEM((4, ATTN, ROWS), BF16),
            dma((4,)),
            dma((4,)),
            dma,
            dma((3,)),
            dma((2,)),
            dma((CHUNKS,)),
            dma((CHUNKS,)),
            dma((CHUNKS,)),
            dma((4,)),
        ],
        compiler_params=pltpu.CompilerParams(
            collective_id=0, has_side_effects=True, vmem_limit_bytes=63 * 1024 * 1024
        ),
        cost_estimate=pl.CostEstimate(
            flops=18_300_000_000, bytes_accessed=28_000_000, transcendentals=300_000
        ),
        name="upsampler",
    )(
        bottom_codes, cond_codes, norm_gain.reshape(WIDTH // 128, 128),
        norm_bias.reshape(WIDTH // 128, 128),
        bottom_table, cond_table, conv_dilated.reshape(3 * CH, CH), conv_mix, projection,
        attn_weight.T,
    )
    return out.transpose(0, 2, 1)


def solution(mesh):
    split = P(None, ("ctx", "seq"))
    return jax.shard_map(
        body,
        mesh=mesh,
        in_specs=(split, split) + (P(),) * 8,
        out_specs=P(None, ("ctx", "seq"), None),
        check_vma=False,
    )
```

time: 76.2 us -> 59.2 us (0.78)
  Pallas kernels: 70.7 us -> 56.8 us
  local copies, waits for them, and re-layouts: 5.2 us -> 2.21 us
    pallas_call x1, Pallas kernels: 70.7 us -> 56.8 us  [body(): pl.pallas_call(kernel, out_shape=jax.ShapeDtypeStruct((4, ATTN, ROWS), BF...]
    reshape x4 -> x0, local copies, waits for them, and re-layouts: 5.2 us -> none  [the longest x1 1.32 us: body(): out = out.reshape(songs, SEQ // 2, 2, COLS, ATTN).transpose(0, 2, 1, 3, 4)]
    unnamed x0 -> x1, local copies, waits for them, and re-layouts: none -> 2.21 us
where the time goes in v2:
time: 59.2 us; the launch traced here: 59 us
  Pallas kernels  56.8 us (96%)
  local copies, waits for them, and re-layouts  2.21 us (4%)
    pallas_call x1, Pallas kernels, body(): pl.pallas_call(kernel, out_shape=jax.ShapeDtypeStruct((4, ATTN, ROWS), BF...  56.8 us
    unnamed x1, local copies, waits for them, and re-layouts  2.21 us

profile of v2, /device:TPU:1, one launch (start us, length us, event | category | flops | bytes accessed | tf_op | source)
XLA Modules:
  0.0 59.0 jit_solution(9077650119778620582)
XLA Ops:
  0.0 56.8 %upsampler.1 = bf16[4,480,256]{2,1,0:T(8,128)(2,1)} custom-call(s32[4,256]{1,0:T(4,128)} %bottom_ref.1, s32[4,64]{1,0:T(4,128)} %cond_ref.1, f32[15,128]{1,0:T(8,128)} %bitcast.8, f32[15,128]{1,0:T(8,128)} %bitcast.9, bf16[2048,1024]{1,0:T(8,128)(2,1)} %btab.1, bf16[2048,1024]{1,0:T(8,128)(2,1)} %ctab.1, bf16[3072,1024]{1,0:T(8,128)(2,1)} %bitcast.6, ...), custom_call_target="tpu_custom_call" | custom-call | flops 18300000256 | bytes 28000000 | tf_op jit(solution)/shard_map/upsampler/pallas_call | solution.py:425
  56.8 2.2 %copy.12 = bf16[4,256,480]{1,2,0:T(8,128)(2,1)} copy(bf16[4,256,480]{1,2,0:T(8,128)(2,1)} %bitcast.5) | data formatting | bytes 1966080

commit v3 on v2

--- a/solution.py
+++ b/solution.py
@@ -38,8 +38,8 @@
     out_ref,
     tb, tc, stage, wconv, wmix, wproj, wattn,
     sendc, codes, gath, gsm,
-    stream, act, lhs, hidden, resid, pj, normed, qkv, att, sendo, got, turned,
-    stage_sem, w_sem, csend_sem, crecv_sem, g_sem, osend_sem, orecv_sem, local_sem, out_sem,
+    stream, act, lhs, hidden, resid, pj, normed, qkv, att, sendo, got,
+    stage_sem, w_sem, csend_sem, crecv_sem, g_sem, osend_sem, orecv_sem, local_sem,
 ):
     a = lax.axis_index("ctx")
     j = lax.axis_index("seq")
@@ -329,7 +329,7 @@
                 sendo[i, d, :, g * 128 : g * 128 + wide] = x[:, :wide].astype(BF16)
             return 0
 
-        lax.fori_loop(0, SEQ, regroup, 0, unroll=8)
+        lax.fori_loop(0, SEQ, regroup, 0, unroll=True)
 
     def send_rows(i):
         s, p = divmod(i, 2)
@@ -389,7 +389,6 @@
     ci = lax.broadcasted_iota(I32, (ROWS, ROWS), 1)
     place = (ri // 8) * COLS + ri % COLS + ((ri // COLS) % 2) * BLOCK
     order = jnp.where(place == ci, 1.0, 0.0).astype(BF16)
-    out_copies = []
     for s in range(2):
         for i in (2 * s, 2 * s + 1):
             view = sendo.at[i, pl.ds(0, SEQ - 1)]
@@ -400,14 +399,9 @@
             ).wait()
         for song in (s, s + 2):
             x = got[song].astype(F32).reshape(ROWS, ATTN).astype(BF16)
-            turned[song] = lax.dot_general(
+            out_ref[song] = lax.dot_general(
                 x, order, (((0,), (0,)), ((), ())), preferred_element_type=F32
             ).astype(BF16)
-            copy = pltpu.make_async_copy(turned.at[song], out_ref.at[song], out_sem.at[song])
-            copy.start()
-            out_copies.append(copy)
-    for copy in out_copies:
-        copy.wait()
     code_wait(SEQ - 1, csend_sem)
 
     @pl.when(jnp.logical_or(to_next, to_prev))
@@ -424,9 +418,9 @@
     dma = pltpu.SemaphoreType.DMA
     out = pl.pallas_call(
         kernel,
-        out_shape=jax.ShapeDtypeStruct((4, ATTN, ROWS), BF16),
+        out_shape=pltpu.VMEM((4, ATTN, ROWS), BF16),
         in_specs=[vmem] * 4 + [hbm] * 6,
-        out_specs=hbm,
+        out_specs=vmem,
         scratch_shapes=[
             pltpu.VMEM((VOCAB * 8 + 8, 128), F32),
             pltpu.VMEM((VOCAB * 8, 128), F32),
@@ -450,7 +444,6 @@
             pltpu.VMEM((4, 8 * CPITCH, 128), F32),
             pltpu.VMEM((CHUNKS, SEQ, 8, ATTN), BF16),
             pltpu.VMEM((4, SEQ // 2, 2, 8, ATTN), BF16),
-            pltpu.VMEM((4, ATTN, ROWS), BF16),
             dma((4,)),
             dma((4,)),
             dma,
@@ -459,7 +452,6 @@
             dma((CHUNKS,)),
             dma((CHUNKS,)),
             dma((CHUNKS,)),
-            dma((4,)),
         ],
         compiler_params=pltpu.CompilerParams(
             collective_id=0, has_side_effects=True, vmem_limit_bytes=63 * 1024 * 1024

time: 59.2 us -> 56.8 us (0.959)
  local copies, waits for them, and re-layouts: 2.21 us -> 0.95 us
  Pallas kernels: 56.8 us -> 55.7 us
    unnamed x1, local copies, waits for them, and re-layouts: 2.21 us -> 0.95 us
    pallas_call x1, Pallas kernels: 56.8 us -> 55.7 us  [body(): pl.pallas_call(kernel, out_shape=pltpu.VMEM((4, ATTN, ROWS), BF16), in_sp...]
where the time goes in v3:
time: 56.8 us; the launch traced here: 56.7 us
  Pallas kernels  55.7 us (98%)
  local copies, waits for them, and re-layouts  0.95 us (2%)
    pallas_call x1, Pallas kernels, body(): pl.pallas_call(kernel, out_shape=pltpu.VMEM((4, ATTN, ROWS), BF16), in_sp...  55.7 us

profile of v3, /device:TPU:1, one launch (start us, length us, event | category | flops | bytes accessed | tf_op | source)
XLA Modules:
  0.0 56.7 jit_solution(17197369780529187066)
XLA Ops:
  0.0 55.7 %upsampler.1 = bf16[4,480,256]{2,1,0:T(8,128)(2,1)S(1)} custom-call(s32[4,256]{1,0:T(4,128)} %bottom_ref.1, s32[4,64]{1,0:T(4,128)} %cond_ref.1, f32[15,128]{1,0:T(8,128)} %bitcast.8, f32[15,128]{1,0:T(8,128)} %bitcast.9, bf16[2048,1024]{1,0:T(8,128)(2,1)} %btab.1, bf16[2048,1024]{1,0:T(8,128)(2,1)} %ctab.1, bf16[3072,1024]{1,0:T(8,128)(2,1)} %bitcast.6, ...), custom_call_target="tpu_custom_call" | custom-call | flops 18300000256 | bytes 28000000 | tf_op jit(solution)/shard_map/upsampler/pallas_call | solution.py:419
  55.8 0.9 %copy.12 = bf16[4,256,480]{1,2,0:T(8,128)(2,1)} copy(bf16[4,256,480]{1,2,0:T(8,128)(2,1)S(1)} %bitcast.5) | data formatting | bytes 1966080

commit v4 on v3

--- a/solution.py
+++ b/solution.py
@@ -347,14 +347,14 @@
             ).start()
             return 0
 
-        lax.fori_loop(1, SEQ, send_out, 0)
+        lax.fori_loop(1, SEQ, send_out, 0, unroll=True)
         pltpu.make_async_copy(sendo.at[i, j], got.at[song, k, p], local_sem.at[i]).start()
 
     def first_rows(e, _):
-        gather_rows(0, e * 4, 4)
+        gather_rows(0, e * 8, 8)
         return 0
 
-    lax.fori_loop(0, BLOCKS // 4, first_rows, 0)
+    lax.fori_loop(0, BLOCKS // 8, first_rows, 0)
     for q in range(4):
         pack_rows(0, q * 64, 64)
 

time: 56.8 us -> 56.6 us (level)
  no operation moved by 1% of the time
where the time goes in v4:
time: 56.6 us; the launch traced here: 56.5 us
  Pallas kernels  55.5 us (98%)
  local copies, waits for them, and re-layouts  0.95 us (2%)
    pallas_call x1, Pallas kernels, body(): pl.pallas_call(kernel, out_shape=pltpu.VMEM((4, ATTN, ROWS), BF16), in_sp...  55.5 us

profile of v4, /device:TPU:1, one launch (start us, length us, event | category | flops | bytes accessed | tf_op | source)
XLA Modules:
  0.0 56.5 jit_solution(16232335710740246074)
XLA Ops:
  0.0 55.5 %upsampler.1 = bf16[4,480,256]{2,1,0:T(8,128)(2,1)S(1)} custom-call(s32[4,256]{1,0:T(4,128)} %bottom_ref.1, s32[4,64]{1,0:T(4,128)} %cond_ref.1, f32[15,128]{1,0:T(8,128)} %bitcast.8, f32[15,128]{1,0:T(8,128)} %bitcast.9, bf16[2048,1024]{1,0:T(8,128)(2,1)} %btab.1, bf16[2048,1024]{1,0:T(8,128)(2,1)} %ctab.1, bf16[3072,1024]{1,0:T(8,128)(2,1)} %bitcast.6, ...), custom_call_target="tpu_custom_call" | custom-call | flops 18300000256 | bytes 28000000 | tf_op jit(solution)/shard_map/upsampler/pallas_call | solution.py:419
  55.5 0.9 %copy.12 = bf16[4,256,480]{1,2,0:T(8,128)(2,1)} copy(bf16[4,256,480]{1,2,0:T(8,128)(2,1)S(1)} %bitcast.5) | data formatting | bytes 1966080

commit v5 on v4

--- a/solution.py
+++ b/solution.py
@@ -351,10 +351,10 @@
         pltpu.make_async_copy(sendo.at[i, j], got.at[song, k, p], local_sem.at[i]).start()
 
     def first_rows(e, _):
-        gather_rows(0, e * 8, 8)
+        gather_rows(0, e * 16, 16)
         return 0
 
-    lax.fori_loop(0, BLOCKS // 8, first_rows, 0)
+    lax.fori_loop(0, BLOCKS // 16, first_rows, 0)
     for q in range(4):
         pack_rows(0, q * 64, 64)
 

time: 56.6 us -> 56.7 us (level)
  no operation moved by 1% of the time
where the time goes in v5:
time: 56.7 us; the launch traced here: 56.5 us
  Pallas kernels  55.6 us (98%)
  local copies, waits for them, and re-layouts  0.95 us (2%)
    pallas_call x1, Pallas kernels, body(): pl.pallas_call(kernel, out_shape=pltpu.VMEM((4, ATTN, ROWS), BF16), in_sp...  55.6 us

profile of v5, /device:TPU:1, one launch (start us, length us, event | category | flops | bytes accessed | tf_op | source)
XLA Modules:
  0.0 56.5 jit_solution(7596705143738885770)
XLA Ops:
  0.0 55.6 %upsampler.1 = bf16[4,480,256]{2,1,0:T(8,128)(2,1)S(1)} custom-call(s32[4,256]{1,0:T(4,128)} %bottom_ref.1, s32[4,64]{1,0:T(4,128)} %cond_ref.1, f32[15,128]{1,0:T(8,128)} %bitcast.8, f32[15,128]{1,0:T(8,128)} %bitcast.9, bf16[2048,1024]{1,0:T(8,128)(2,1)} %btab.1, bf16[2048,1024]{1,0:T(8,128)(2,1)} %ctab.1, bf16[3072,1024]{1,0:T(8,128)(2,1)} %bitcast.6, ...), custom_call_target="tpu_custom_call" | custom-call | flops 18300000256 | bytes 28000000 | tf_op jit(solution)/shard_map/upsampler/pallas_call | solution.py:419
  55.6 0.9 %copy.12 = bf16[4,256,480]{1,2,0:T(8,128)(2,1)} copy(bf16[4,256,480]{1,2,0:T(8,128)(2,1)S(1)} %bitcast.5) | data formatting | bytes 1966080
